TPU v7x, 128 devices: a whole 4x4x4 slice. The times are simulated.
128 devices in a mesh: dp: 8 (over z, core), tensor: 16 (over x, y).
Axes of the slice: x: 4, y: 4, z: 4, core: 2. Of those that a mesh axis runs over, the one named last changes fastest.
Arguments:
- queries: bfloat16 [512, 6144], P('dp', 'tensor'), may hold values from -4.5 to 4.5
- key_cache: bfloat16 [512, 16, 128, 128], P('dp', 'tensor'), may hold values from -4.5 to 4.5
- value_cache: bfloat16 [512, 16, 128, 128], P('dp', 'tensor'), may hold values from -6 to 6
- lengths: int32 [512], P('dp'), may hold values from 2 to 128, as said below
- out_proj: bfloat16 [6144, 6144], P('tensor'), may hold values from -0.75 to 0.75
- residual: bfloat16 [512, 6144], P('dp'), may hold values from -6 to 6
- norm_gain: bfloat16 [6144], replicated, may hold values from 0.099609375 to 1.8984375
- expert_ids: int32 [512, 2], P('dp'), may hold values from 0 to 7, all different within a row; in each aligned block of 64 rows (0 to 63, 64 to 127, ...) at most 24 rows name the same one
- gate_weights: float32 [512, 2], P('dp'), may hold values from 0.2 to 1
- w_gate: bfloat16 [8, 6144, 8192], P('dp', None, 'tensor'), may hold values from -0.078125 to 0.078125
- w_up: bfloat16 [8, 6144, 8192], P('dp', None, 'tensor'), may hold values from -0.078125 to 0.078125
- w_down: bfloat16 [8, 8192, 6144], P('dp', 'tensor'), may hold values from -0.09375 to 0.09375
Outputs:
- layer_out: bfloat16 [512, 6144], P('dp', 'tensor')
Inputs may be any that keep to these rules, and one draw needn't show every extreme that they name: Row r uses cache positions 0 to lengths[r] - 1; in every aligned block of 64 rows some row has exactly 128. `expert_ids`: each row names two different experts; within each aligned block of 64 rows no expert is named by more than 24 rows, a bound that some block reaches.
All inputs are finite; a program needn't handle non-finite values.
Results may differ from a plain program's by a relative error of at most 0.0059.
Values may be sent and summed in bfloat16 or wider, within the bound.
A program may use at most 128 MiB of HBM per device.

v0:
```python
import jax
import jax.numpy as jnp
from jax import lax
from jax.sharding import PartitionSpec as P

HD = 128


epsilon = 1e-05


def build_slots(expert_ids, experts, capacity):
    flat_ids = expert_ids.reshape(-1)
    onehot = (flat_ids[:, None] == jnp.arange(experts)[None, :]).astype(jnp.int32)
    earlier = jnp.cumsum(onehot, axis=0) - onehot
    position = jnp.sum(earlier * onehot, axis=1)
    target = flat_ids * capacity + position
    return (target[None, :] == jnp.arange(experts * capacity)[:, None]).astype(jnp.bfloat16)


def attend(queries, key_cache, value_cache, lengths):
    row_count = queries.shape[0]
    local_heads = queries.shape[1] // HD
    query_grid = queries.reshape(row_count, 1, local_heads, HD)
    scores = jnp.einsum(
        "rsgd,rscd->rsgc", query_grid, key_cache, preferred_element_type=jnp.float32
    ) * HD ** (-0.5)
    visible = jnp.arange(key_cache.shape[2])[None, :] < lengths[:, None]
    scores = jnp.where(visible[:, None, None, :], scores, -1e30)
    row_max = jnp.max(scores, axis=-1, keepdims=True)
    exp_scores = jnp.exp(scores - row_max)
    weights = (exp_scores / jnp.sum(exp_scores, axis=-1, keepdims=True)).astype(jnp.bfloat16)
    combined = jnp.einsum(
        "rsgc,rscd->rsgd", weights, value_cache, preferred_element_type=jnp.float32
    )
    return combined.astype(jnp.bfloat16).reshape(row_count, local_heads * HD)


def local(
    queries,
    key_cache,
    value_cache,
    lengths,
    out_proj,
    residual,
    norm_gain,
    expert_ids,
    gate_weights,
    w_gate,
    w_up,
    w_down,
):
    attended = attend(queries, key_cache, value_cache, lengths)
    partial_value = jnp.dot(attended, out_proj, preferred_element_type=jnp.float32)
    row_count = partial_value.shape[0]
    model_width = partial_value.shape[1]
    tensor_count = lax.axis_size("tensor")
    share_width = model_width // tensor_count
    offset = lax.axis_index("tensor") * share_width
    experts = lax.axis_size("dp")
    capacity = 3 * row_count // experts
    slot_table = build_slots(expert_ids, experts, capacity)
    gate_mat = w_gate[0]
    up_mat = w_up[0]
    down_mat = w_down[0]
    hidden = residual.astype(jnp.float32) + lax.psum(partial_value, "tensor")
    inverse = lax.rsqrt(jnp.mean(hidden * hidden, axis=1, keepdims=True) + epsilon)
    normed = (hidden * inverse * norm_gain.astype(jnp.float32)).astype(jnp.bfloat16)
    hidden_share = lax.dynamic_slice_in_dim(hidden, offset, share_width, 1)
    outgoing = jnp.dot(
        slot_table, jnp.repeat(normed, 2, axis=0), preferred_element_type=jnp.float32
    )
    outgoing = outgoing.astype(jnp.bfloat16).reshape(experts, capacity, model_width)
    arrived = lax.all_to_all(outgoing, "dp", split_axis=0, concat_axis=0, tiled=True).reshape(
        experts * capacity, model_width
    )
    gate_value = jnp.dot(arrived, gate_mat, preferred_element_type=jnp.float32)
    up_value = jnp.dot(arrived, up_mat, preferred_element_type=jnp.float32)
    active = (jax.nn.silu(gate_value) * up_value).astype(jnp.bfloat16)
    expert_terms = jnp.dot(active, down_mat, preferred_element_type=jnp.float32)
    result = lax.psum_scatter(expert_terms, "tensor", scatter_dimension=1, tiled=True).astype(
        jnp.bfloat16
    )
    returned = lax.all_to_all(
        result.reshape(experts, capacity, share_width),
        "dp",
        split_axis=0,
        concat_axis=0,
        tiled=True,
    )
    returned = returned.reshape(experts * capacity, share_width)
    per_slot = jnp.einsum("pa,pw->aw", slot_table, returned, preferred_element_type=jnp.float32)
    per_slot = per_slot.reshape(row_count, 2, share_width)
    layer_out = hidden_share + jnp.sum(gate_weights[:, :, None] * per_slot, axis=1)
    return layer_out.astype(jnp.bfloat16)


def solution(mesh):
    placed = (
        P("dp", "tensor"),
        P("dp", "tensor", None, None),
        P("dp", "tensor", None, None),
        P("dp"),
        P("tensor", None),
        P("dp", None),
        P(),
        P("dp", None),
        P("dp", None),
        P("dp", None, "tensor"),
        P("dp", None, "tensor"),
        P("dp", "tensor", None),
    )
    return jax.shard_map(
        local, mesh=mesh, in_specs=placed, out_specs=P("dp", "tensor"), check_vma=False
    )
```

profile of v0, /device:TPU:1, one launch (start us, length us, event | category | flops | bytes accessed | tf_op | source)
XLA Modules:
  0.0 267.4 jit_solution(4208251601772111389)
XLA Ops:
  6.5 0.0 copy-start
  6.5 0.0 all-reduce.2.cloned.1.call-start
  6.5 1.0 reshape.111
  7.5 0.7 iota_compare_fusion.4
  8.2 0.0 copy-done
  8.3 1.2 fusion.23
  9.4 0.2 fusion.47
  9.7 2.5 fusion.26
  12.2 0.0 copy-start.4
  12.2 0.0 copy-start.5
  12.2 4.5 %fusion.42 = f32[64,6144]{1,0:T(8,128)} fusion(bf16[384,6144]{1,0:T(8,128)(2,1)} %param.16, bf16[8,8,3,128]{3,2,1,0:T(4,128)(2,1)S(1)} %bitcast.52), kind=kOutput, calls=%fused_computation.40 | convolution fusion | flops 301989888 | bytes 6340608 | tf_op jit(solution)/shard_map/dot_general | solution.py:54
  16.7 0.0 copy-start.3
  16.7 0.0 all-reduce.2.cloned.1.call-update
  16.7 0.0 reduce-scatter.2.cloned.1.call-start
  16.7 0.0 copy-done.4
  16.8 0.0 copy-done.5
  16.8 0.1 copy.21
  16.9 0.1 reshape.115
  17.0 0.1 fusion.40
  17.1 0.2 reduce_window_sum.11
  17.3 0.2 select_reduce_fusion
  17.5 89.6 %all-reduce.2.cloned.1.call-done = f32[64,6144]{1,0:T(8,128)} async-done(((f32[64,6144]{1,0:T(8,128)}), f32[64,6144]{1,0:T(8,128)}) %all-reduce.2.cloned.1.call-update) | async-done | bytes 1572880 | tf_op jit(solution)/shard_map/psum | solution.py:66
  107.1 0.0 copy-done.3
  107.1 1.7 multiply_reduce_fusion
  108.8 0.0 copy-start.2
  108.8 1.2 copy-done.2
  110.0 0.2 multiply_convert_fusion
  110.2 2.1 broadcast_in_dim.16
  112.3 4.5 %reshape.116 = bf16[128,6144]{1,0:T(8,128)(2,1)} reshape(bf16[64,2,6144]{2,1,0:T(2,128)(2,1)} %broadcast_in_dim.16) | data formatting | bytes 3145728 | tf_op jit(solution)/shard_map/reshape | solution.py:71
  116.8 2.2 convolution_convert_fusion
  119.0 35.7 %all_to_all.10 = bf16[8,24,6144]{2,1,0:T(8,128)(2,1)S(1)} all-to-all(bf16[8,24,6144]{2,1,0:T(8,128)(2,1)S(1)} %bitcast.50), channel_id=1, replica_groups=mesh['dp'=8,'tensor'=16] {'dp'}, dimensions={0} | all-to-all | bytes 4718592 | tf_op jit(solution)/shard_map/all_to_all | solution.py:74
  154.7 0.0 copy-start.1
  154.7 1.4 copy-done.1
  156.1 4.2 %fusion.5 = f32[192,512]{1,0:T(8,128)S(1)} fusion(bf16[192,6144]{1,0:T(8,128)(2,1)S(1)} %bitcast.48, bf16[1,6144,512]{2,1,0:T(8,128)(2,1)} %param.21), kind=kOutput, calls=%fused_computation.6 | convolution fusion | flops 1207959552 | bytes 9043968 | tf_op jit(solution)/shard_map/dot_general | solution.py:77
  160.3 10.1 %fusion.1 = f32[192,6144]{1,0:T(8,128)} fusion(bf16[1,512,6144]{2,1,0:T(8,128)(2,1)} %param.23, bf16[192,6144]{1,0:T(8,128)(2,1)} %bitcast.49, bf16[1,6144,512]{2,1,0:T(8,128)(2,1)} %param.22, f32[192,512]{1,0:T(8,128)S(1)} %fusion.5), kind=kOutput, calls=%fused_computation.2 | convolution fusion | flops 2416508928 | bytes 20054016 | tf_op jit(solution)/shard_map/dot_general | solution.py:80
  170.4 0.0 copy-start.6
  170.4 0.0 reduce-scatter.2.cloned.1.call-update
  170.5 0.1 reduce_sum.40
  170.6 0.1 copy.22
  170.7 74.3 %reduce-scatter.2.cloned.1.call-done = f32[192,384]{1,0:T(8,128)} async-done(((f32[192,6144]{1,0:T(8,128)}), f32[192,384]{1,0:T(8,128)}) %reduce-scatter.2.cloned.1.call-update) | async-done | bytes 294928 | tf_op jit(solution)/shard_map/reduce_scatter | solution.py:81
  245.0 1.6 convert_element_type.41
  246.6 6.7 %all-to-all-start.1 = ((bf16[8,24,384]{2,1,0:T(8,128)(2,1)}), bf16[8,24,384]{2,1,0:T(8,128)(2,1)S(1)}, u32[]{:S(2)}, u32[]{:S(2)}) async-start(bf16[8,24,384]{2,1,0:T(8,128)(2,1)} %bitcast.8), calls=%async_computation.2 | async-start | bytes 294912 | tf_op jit(solution)/shard_map/all_to_all | solution.py:84
  253.3 5.4 %all-to-all-done.1 = bf16[8,24,384]{2,1,0:T(8,128)(2,1)S(1)} async-done(((bf16[8,24,384]{2,1,0:T(8,128)(2,1)}), bf16[8,24,384]{2,1,0:T(8,128)(2,1)S(1)}, u32[]{:S(2)}, u32[]{:S(2)}) %all-to-all-start.1) | async-done | bytes 147488 | tf_op jit(solution)/shard_map/all_to_all | solution.py:84
  258.8 0.0 copy-done.6
  258.8 0.2 fusion.18
  259.0 1.5 add_convert_fusion
  (4 shorter events, 0.0 us)
Async XLA Ops:
  6.5 1.7 copy-start
  6.5 100.5 %all-reduce.2.cloned.1.call-start = ((), (), s32[]{:S(2)}) async-start(), calls=%async_computation.3 | async-start | bytes 3145728 | tf_op jit(solution)/shard_map/psum | solution.py:66
  12.2 4.6 %copy-start.4 = (bf16[6144]{0:T(1024)(128)(2,1)S(1)}, bf16[6144]{0:T(1024)(128)(2,1)}, u32[]{:S(2)}) copy-start(bf16[6144]{0:T(1024)(128)(2,1)} %param.18) | copy-start | bytes 36868
  12.2 4.6 %copy-start.5 = (s32[64,2]{0,1:T(2,128)S(1)}, s32[64,2]{0,1:T(2,128)}, u32[]{:S(2)}) copy-start(s32[64,2]{0,1:T(2,128)} %param.19) | copy-start | bytes 1540
  16.7 90.4 %copy-start.3 = (bf16[64,6144]{1,0:T(8,128)(2,1)S(1)}, bf16[64,6144]{1,0:T(8,128)(2,1)}, u32[]{:S(2)}) copy-start(bf16[64,6144]{1,0:T(8,128)(2,1)} %param.17) | copy-start | bytes 2359300
  16.7 228.3 %reduce-scatter.2.cloned.1.call-start = ((), (), s32[]{:S(2)}) async-start(), calls=%async_computation.4 | async-start | bytes 5013504 | tf_op jit(solution)/shard_map/reduce_scatter | solution.py:81
  108.8 1.2 copy-start.2
  154.7 1.4 copy-start.1
  170.4 88.3 %copy-start.6 = (f32[64,2]{0,1:T(2,128)S(1)}, f32[64,2]{0,1:T(2,128)}, u32[]{:S(2)}) copy-start(f32[64,2]{0,1:T(2,128)} %param.20) | copy-start | bytes 1540
  246.6 12.1 %all-to-all-start.1 = ((bf16[8,24,384]{2,1,0:T(8,128)(2,1)}), bf16[8,24,384]{2,1,0:T(8,128)(2,1)S(1)}, u32[]{:S(2)}, u32[]{:S(2)}) async-start(bf16[8,24,384]{2,1,0:T(8,128)(2,1)} %bitcast.8), calls=%async_computation.2 | async-start | bytes 294912 | tf_op jit(solution)/shard_map/all_to_all | solution.py:84
Sparse Core Ops, SparseCore 0:
  16.8 90.2 all-reduce.1
  170.6 74.3 reduce-scatter.1
where the time goes:
time: 268 us; the launch traced here: 267 us
  waiting for transfers between devices  169 us (63%)
  blocking collectives  35.7 us (13%)
  matrix products  24.9 us (9%)
  between operations  13.5 us (5%)
  local copies, waits for them, and re-layouts  10.6 us (4%)
  starting transfers between devices  6.74 us (3%)
  other arithmetic  6.54 us (2%)
    psum x1, waiting for transfers between devices, local(): hidden = residual.astype(jnp.float32) + lax.psum(partial_value, 'tensor')  89.6 us
    reduce_scatter x1, waiting for transfers between devices, local(): lax.psum_scatter(expert_terms, 'tensor', scatter_dimension=1, tiled=True)  74.3 us
    all_to_all x1, blocking collectives, local(): lax.all_to_all(outgoing, 'dp', split_axis=0, concat_axis=0, tiled=True)  35.7 us
    dot_general x1, matrix products, local(): expert_terms = jnp.dot(active, down_mat, preferred_element_type=jnp.float32)  10.1 us
    all_to_all x1, starting transfers between devices, local(): lax.all_to_all(result.reshape(experts, capacity, share_width), 'dp', spli...  6.7 us
    all_to_all x1, waiting for transfers between devices, local(): lax.all_to_all(result.reshape(experts, capacity, share_width), 'dp', spli...  5.42 us
  transfers between devices with their start and end apart: 3, of which 3 were waited for; matrix products, arithmetic and copies ran while one was open for 0% of the time, Pallas kernels for 0%

commit v1 on v0

v1 whole, which is shorter than its diff:
```python
import math

import jax
import jax.numpy as jnp
from jax import lax
from jax.experimental import pallas as pl
from jax.experimental.pallas import tpu as pltpu
from jax.sharding import PartitionSpec as P

HD = 128
CAP = 24
PAD = 32
EPSILON = 1e-05
F32 = jnp.float32
BF16 = jnp.bfloat16
N_SEMS = 8 + 28 + 36 + 1 + 1

ORDER = (
    (2, 2), (1, 2), (3, 2), (2, 1), (2, 3), (1, 1), (1, 3), (3, 1), (3, 3),
    (2, 0), (0, 2), (1, 0), (3, 0), (0, 1), (0, 3), (0, 0),
)


class Links:
    def __init__(self, send_sem, recv_sem, to):
        self.send_sem, self.recv_sem, self.to = send_sem, recv_sem, to
        self.sent = 0
        self.numbers = {}

    def copy(self, key, src, dst, where):
        number = self.numbers.setdefault(key, len(self.numbers))
        return pltpu.make_async_remote_copy(
            src_ref=src,
            dst_ref=dst,
            send_sem=self.send_sem.at[0],
            recv_sem=self.recv_sem.at[number],
            device_id=self.to[where],
            device_id_type=pl.DeviceIdType.MESH,
        )

    def send(self, key, src, dst, where):
        self.copy(key, src, dst, where).start()
        self.sent += math.prod(src.shape)

    def arrived(self, key, dst):
        self.copy(key, dst, dst, "x+").wait_recv()

    def finish(self, space):
        space = space.at[pl.ds(0, self.sent // space.shape[1])]
        self.copy(next(iter(self.numbers)), space, space, "x+").wait_send()


def f32(value):
    return value.astype(F32)


class Quarter:
    def __init__(self, links, index, rows, axes, side):
        self.links, self.index, self.axes, self.side = links, index, axes, side
        self.rows = pl.ds(index * rows, rows)

    def place(self, first, second):
        return (first, second) if self.axes[0] == "x" else (second, first)

    def where(self, step, side):
        return self.axes[step] + side

    def key(self, *name):
        return (self.index, *name)


class Gather(Quarter):
    def __init__(self, held, *others):
        super().__init__(*others)
        self.held = held

    def at(self, place):
        return self.held.at[place[0], place[1], self.rows]

    def send(self, step, side, first, second, name):
        shift = 3 if side == "+" else 1
        there = ((first + shift) % 4, second) if step == 0 else (first, (second + shift) % 4)
        key = ("g", name, first) if name == "last" else self.key("g", name, first)
        self.links.send(
            key, self.at(self.place(first, second)), self.at(self.place(*there)),
            self.where(step, side),
        )

    def arrived(self, name, d, count=1):
        rows = self.rows.size
        self.links.arrived(self.key("g", name, d), self.held.at[0, 0, pl.ds(0, count * rows)])

    def spread(self, d):
        for side in "+-":
            self.send(1, side, d, 0, "spread")

    def pass_on(self, d):
        self.arrived("spread", d, 2)
        self.send(1, self.side, d, 3 if self.side == "+" else 1, "last")

    def own(self):
        for side in "+-":
            self.send(0, side, 0, 0, "own")
        two_away = self.at(self.place(2, 0))
        self.links.send(self.key("g", "far"), self.at(self.place(0, 0)), two_away, (self.axes[0], 2))
        self.spread(0)

    def near(self):
        self.arrived("own", 0, 2)
        self.spread(3)
        self.spread(1)

    def far(self):
        self.links.arrived(self.key("g", "far"), self.at(self.place(2, 0)))
        self.spread(2)


class Sum(Quarter):
    def __init__(self, part, far1, near1, near2, *others):
        super().__init__(*others)
        self.part, self.far1, self.near1, self.near2 = part, far1, near1, near2
        self.near, self.other, self.opposite = (1, 3, "-") if self.side == "+" else (3, 1, "+")

    def at(self, first, second):
        i, j = self.place(first, second)
        return self.part.at[i, j, self.rows]

    def load(self, first, second):
        i, j = self.place(first, second)
        return f32(self.part[i, j, self.rows, :])

    def store(self, first, second, value):
        i, j = self.place(first, second)
        self.part[i, j, self.rows, :] = value.astype(BF16)

    def slot(self, side):
        return 0 if side == "+" else 1

    def forward(self, d):
        self.links.send(self.key("s", "far", d), self.at(d, 2), self.far1.at[self.index, d], self.where(1, self.side))

    def direct(self, d):
        there = self.near1.at[self.index, self.slot(self.opposite), d]
        self.links.send(self.key("s", "near", d), self.at(d, self.other), there, self.where(1, self.opposite))

    def joined(self, d):
        here = self.far1.at[self.index, d]
        self.links.arrived(self.key("s", "far", d), here)
        self.store(d, self.near, self.load(d, self.near) + f32(here[...]))
        there = self.near1.at[self.index, self.slot(self.side), d]
        self.links.send(self.key("s", "near", d), self.at(d, self.near), there, self.where(1, self.side))

    def first_sum(self, d):
        self.links.arrived(self.key("s", "near", d), self.near1.at[self.index, :, d])
        total = self.load(d, 0) + f32(self.near1[self.index, 0, d]) + f32(self.near1[self.index, 1, d])
        if d:
            self.store(d, 0, total)
            there = self.near2.at[self.index, d - 1]
            self.links.send(self.key("s", "near2"), self.at(d, 0), there, (self.axes[0], d))
        else:
            self.own_sum = total

    def result(self):
        self.links.arrived(self.key("s", "near2"), self.near2.at[self.index])
        total = self.own_sum
        for n in range(3):
            total = total + f32(self.near2[self.index, n])
        return total


class PlaneSum:
    def __init__(self, links, index, part, first, staged, second, y):
        self.links, self.index, self.part, self.y = links, index, part, y
        self.first, self.staged, self.second = first, staged, second
        step = part.shape[2] // 4
        self.a, self.b = pl.ds(2 * index * step, step), pl.ds((2 * index + 1) * step, step)

    def start(self):
        for n, d in enumerate((2, 1, 3)):
            self.links.send(
                ("p1a", self.index), self.part.at[:, (self.y + d) % 4, self.a], self.first.at[self.index, 0, n], ("y", d)
            )
            self.links.send(("p1b", self.index), self.part.at[d, :, self.b], self.first.at[self.index, 1, n], ("x", d))

    def second_step(self):
        totals = f32(self.part[:, pl.ds(self.y, 1), self.a, :][:, 0]), f32(self.part[0, :, self.b, :])
        for kind in range(2):
            total = totals[kind]
            self.links.arrived(("p1" + "ab"[kind], self.index), self.first.at[self.index, kind])
            for n in range(3):
                total = total + f32(self.first[self.index, kind, n])
            self.staged[self.index, kind] = total.astype(BF16)
            for n, d in enumerate((2, 1, 3)):
                other = d if kind == 0 else (self.y + d) % 4
                self.links.send(
                    ("p2" + "ab"[kind], self.index), self.staged.at[self.index, kind, other],
                    self.second.at[self.index, kind, n], ("xy"[kind], d),
                )

    def result(self):
        out = []
        for kind in range(2):
            total = f32(self.staged[self.index, 0, 0]) if kind == 0 else f32(self.staged[self.index, 1, self.y])
            self.links.arrived(("p2" + "ab"[kind], self.index), self.second.at[self.index, kind])
            for n in range(3):
                total = total + f32(self.second[self.index, kind, n])
            out.append(total)
        return out


def column_of(line):
    count = line.shape[1]
    shape = (count, count)
    diagonal = lax.broadcasted_iota(jnp.int32, shape, 0) == lax.broadcasted_iota(jnp.int32, shape, 1)
    return jnp.sum(jnp.where(diagonal, line, 0.0), axis=1, keepdims=True)


def attend(queries, keys, values, lengths, wait, index):
    width = queries.shape[1]
    heads = width // HD
    step = 16
    cache = keys.shape[1]
    own = lax.broadcasted_iota(jnp.int32, (heads * step, cache), 0) % step
    position = f32(lax.broadcasted_iota(jnp.int32, (heads * step, cache), 1))
    half_blocks = queries.shape[0] // step // 2
    blocks = range(index * half_blocks, (index + 1) * half_blocks)
    if index:
        wait("k", index)
    every = []
    for n in blocks:
        rows = slice(n * step, (n + 1) * step)
        query = queries[rows, :]
        query = jnp.concatenate([query[:, h * HD:(h + 1) * HD] for h in range(heads)], axis=0)
        every.append(lax.dot_general(
            query, keys[rows].reshape(step * cache, HD), (((1,), (1,)), ((), ())), preferred_element_type=F32
        ))
    spread = []
    for n, products in zip(blocks, every):
        scores = products[:, 0:cache]
        for r in range(1, step):
            scores = jnp.where(own == r, products[:, r * cache:(r + 1) * cache], scores)
        scores = scores * HD ** (-0.5)
        length = jnp.concatenate([lengths[n * step:(n + 1) * step]] * heads, axis=0)
        scores = jnp.where(position < length, scores, -1e30)
        exp_scores = jnp.exp(scores - jnp.max(scores, axis=1, keepdims=True))
        weights = exp_scores / jnp.sum(exp_scores, axis=1, keepdims=True)
        spread.append(jnp.concatenate([jnp.where(own == r, weights, 0.0).astype(BF16) for r in range(step)], axis=1))
    wait("v", index)
    out = []
    for n, weights in zip(blocks, spread):
        rows = slice(n * step, (n + 1) * step)
        combined = jnp.dot(weights, values[rows].reshape(step * cache, HD), preferred_element_type=F32).astype(BF16)
        out.append(jnp.concatenate([combined[h * step:(h + 1) * step] for h in range(heads)], axis=1))
    return jnp.concatenate(out, axis=0)


def kernel(
    queries, keys_hbm, values_hbm, lengths, wo_hbm, res_hbm, gain, expert_ids, gate_weights, wg_hbm, wu_hbm, wd_hbm, out,
    keys, values, wo, wg, wu, wd, res,
    part1, first1, second1, staged1,
    part2, far1, near1, near2,
    held, to_send, landed, back, returned, rows_f32, acc_gate, acc_up, squares, act,
    load_sem, send_sem, recv_sem,
):
    group = lax.axis_index("dp")
    tensor = lax.axis_index("tensor")
    x, y = tensor // 4, tensor % 4
    row_count, share = out.shape
    wide = 4 * share

    def at(i, j):
        return ((x + i) % 4) * 4 + (y + j) % 4

    to = {}
    for d in (1, 2, 3):
        to["x", d] = (group, at(d, 0))
        to["y", d] = (group, at(0, d))
    z, core = group // 2, group % 2
    for k in range(1, 8):
        to[k] = (((z + k // 2) % 4) * 2 + (core + k) % 2, tensor)
    barrier = pltpu.get_barrier_semaphore()
    for where in to:
        pl.semaphore_signal(barrier, inc=1, device_id=to[where], device_id_type=pl.DeviceIdType.MESH)
    peers = len(to)
    for name in ("x", "y"):
        to[name + "+"], to[name + "-"] = to[name, 1], to[name, 3]
    links = Links(send_sem, recv_sem, to)

    loads = {}

    def load(key, src, dst):
        pltpu.make_async_copy(src, dst, load_sem.at[loads.setdefault(key, len(loads))]).start()

    def wait(key, whole):
        pltpu.make_async_copy(whole, whole, load_sem.at[loads[key]]).wait()

    def columns(i):
        return pl.ds(pl.multiple_of(((x + i) % 4) * wide, 128), wide)

    def block_rows(i, j):
        return pl.ds(pl.multiple_of(i * wide + ((y + j) % 4) * share, 128), share)

    def block(j):
        return pl.ds(pl.multiple_of(((y + j) % 4) * share, 128), share)

    def cached(name, index):
        array = keys if name == "k" else values
        return array.at[pl.ds(index * half, half)]

    def load_cache(index):
        for name, array in (("k", keys_hbm), ("v", values_hbm)):
            load((name, index), array.at[pl.ds(index * half, half), 0], cached(name, index))

    def wait_cache(name, index):
        wait((name, index), cached(name, index))

    half = row_count // 2
    load_cache(0)
    wait_cache("k", 0)
    for i in range(4):
        load("wo", wo_hbm.at[:, columns(i)], wo.at[i])
    load_cache(1)
    load("res", res_hbm.at[:, pl.ds(pl.multiple_of(tensor * share, 128), share)], res)

    length_column = column_of(f32(lengths[...]))
    halves = [PlaneSum(links, index, part1, first1, staged1, second1, y) for index in range(2)]

    def project(attended, index):
        for i in (2, 1, 3, 0):
            product = jnp.dot(attended, wo[i], preferred_element_type=F32).astype(BF16)
            for j in range(4):
                part1[i, j, index * half:(index + 1) * half, :] = product[:, j * share:(j + 1) * share]

    attended = attend(queries, keys, values, length_column, wait_cache, 0)
    wait("wo", wo)
    project(attended, 0)
    pl.semaphore_wait(barrier, peers)
    halves[0].start()
    project(attend(queries, keys, values, length_column, wait_cache, 1), 1)
    halves[1].start()

    for i in (0, 3, 1, 2):
        load("wg", wg_hbm.at[0, columns(i)], wg.at[pl.ds(i * wide, wide)])
        load("wu", wu_hbm.at[0, columns(i)], wu.at[pl.ds(i * wide, wide)])
    for i in (2, 1, 3, 0):
        load("wd", wd_hbm.at[0, :, columns(i)], wd.at[i])

    def slot_tables():
        slots = 8 * PAD
        ids = expert_ids[...]
        relative = f32((ids // 2 - z + 4) % 4 * 2 + (ids + core) % 2)
        column = lax.broadcasted_iota(jnp.int32, (row_count, slots), 1)
        expert = f32(column // PAD)
        first = jnp.where(column_of(relative[0:1]) == expert, 1.0, 0.0)
        second = jnp.where(column_of(relative[1:2]) == expert, 1.0, 0.0)
        named = first + second
        earlier = jnp.where(
            lax.broadcasted_iota(jnp.int32, (row_count, row_count), 1)
            < lax.broadcasted_iota(jnp.int32, (row_count, row_count), 0),
            1.0,
            0.0,
        )
        rank = jnp.dot(earlier.astype(BF16), named.astype(BF16), preferred_element_type=F32)
        place = jnp.where(rank == f32(column % PAD), 1.0, 0.0)
        acc_gate[...] = jnp.zeros_like(acc_gate)
        acc_up[...] = jnp.zeros_like(acc_up)
        squares[...] = jnp.zeros_like(squares)
        return [(rows * place).astype(BF16) for rows in (first, second, named)]

    first, second, chosen = slot_tables()
    first_weight, second_weight = column_of(gate_weights[0:1]), column_of(gate_weights[1:2])
    for each in halves:
        each.second_step()
    summed = jnp.concatenate(halves[0].result() + halves[1].result(), axis=0)
    wait("res", res)
    hidden = summed + f32(res[...])
    picked = lax.dot_general(
        chosen, hidden.astype(BF16), (((0,), (0,)), ((), ())), preferred_element_type=F32
    )
    to_send[...] = picked.astype(BF16).reshape(8, PAD, share)

    for k in (2, 3, 6, 7, 1, 4, 5):
        links.send("d", to_send.at[k], landed.at[k - 1], k)
    quarter = 2 * CAP
    gathers = [
        Gather(held, links, index, quarter, axes, side)
        for index, (axes, side) in enumerate((("xy", "+"), ("yx", "+"), ("yx", "-"), ("xy", "-")))
    ]

    rows_f32[0:CAP, :] = f32(to_send[0])[:CAP]
    links.arrived("d", landed)
    for k in range(1, 8):
        rows_f32[k * CAP:(k + 1) * CAP, :] = f32(landed[k - 1])[:CAP]
    held[0, 0] = rows_f32[...].astype(BF16)

    def consume(i, j):
        values_f32 = f32(held[i, j])
        square = values_f32 * values_f32
        folded = square[:, 0:128]
        for c in range(1, share // 128):
            folded = folded + square[:, c * 128:(c + 1) * 128]
        squares[...] += folded
        scaled = (values_f32 * f32(gain[0:1, pl.ds(pl.multiple_of(at(i, j) * share, 128), share)])).astype(BF16)
        acc_gate[...] += jnp.dot(scaled, wg[block_rows(i, j), :], preferred_element_type=F32)
        acc_up[...] += jnp.dot(scaled, wu[block_rows(i, j), :], preferred_element_type=F32)

    for each in gathers:
        each.own()
    wait("wg", wg)
    wait("wu", wu)
    consume(0, 0)
    for each in gathers:
        each.near()
    for each in gathers:
        each.pass_on(0)
    for each in gathers:
        each.far()
    for i, j in ((3, 0), (0, 3), (1, 0), (0, 1)):
        consume(i, j)
    for d in (3, 1):
        for each in gathers:
            each.pass_on(d)
    for i, j in ((3, 3), (1, 3), (3, 1), (1, 1)):
        consume(i, j)
    for each in gathers:
        each.pass_on(2)
    for d in (0, 3, 1):
        links.arrived(("g", "last", d), held.at[d, 2])
        consume(d, 2)
        consume(2, d)
    links.arrived(("g", "last", 2), held.at[2, 2])
    consume(2, 2)

    mean = jnp.sum(squares[...], axis=1, keepdims=True) * (1.0 / (16 * share))
    inverse = lax.rsqrt(mean + EPSILON)
    gate = acc_gate[...] * inverse
    up = acc_up[...] * inverse
    act[...] = (gate / (1.0 + jnp.exp(-gate)) * up).astype(BF16)
    wait("wd", wd)

    def down(i, j):
        part2[i, j] = jnp.dot(act[...], wd[i, :, block(j)], preferred_element_type=F32).astype(BF16)

    sums = [
        Sum(part2, far1, near1, near2, links, index, quarter, axes, side)
        for index, (axes, side) in enumerate((("yx", "-"), ("yx", "+"), ("xy", "+"), ("xy", "-")))
    ]
    for i, j in ORDER:
        down(i, j)
        for each in sums:
            d, along = each.place(i, j)
            if along == 2:
                each.forward(d)
    for d in (2, 1, 3, 0):
        for each in sums:
            each.joined(d)
            each.direct(d)
    for d in (2, 3, 1, 0):
        for each in sums:
            each.first_sum(d)

    empty = jnp.zeros((PAD - CAP, share), F32)

    def give_back(each):
        total = each.result()
        for k in (2 * each.index, 2 * each.index + 1):
            first_row = (k % 2) * CAP
            slot = jnp.concatenate([total[first_row:first_row + CAP], empty], axis=0).astype(BF16)
            if k == 0:
                returned[0] = slot
            else:
                back[k] = slot
                links.send("b", back.at[k], returned.at[k], (4 - k // 2) % 4 * 2 + k % 2)

    for index in (2, 3, 1, 0):
        give_back(sums[index])
    links.finish(wg)
    links.arrived("b", returned.at[pl.ds(1, 7)])
    results = returned[...].reshape(8 * PAD, share)
    layer_out = (
        hidden
        + first_weight * jnp.dot(first, results, preferred_element_type=F32)
        + second_weight * jnp.dot(second, results, preferred_element_type=F32)
    )
    out[...] = layer_out.astype(out.dtype)


def local(
    queries, key_cache, value_cache, lengths, out_proj, residual, norm_gain, expert_ids, gate_weights,
    w_gate, w_up, w_down,
):
    rows, share = queries.shape
    cache = key_cache.shape[2]
    hidden_units = w_gate.shape[2]
    slots = 8 * CAP
    vmem = pl.BlockSpec(memory_space=pltpu.VMEM)
    hbm = pl.BlockSpec(memory_space=pl.ANY)
    quarter = slots // 4
    step = rows // 4

    return pl.pallas_call(
        kernel,
        out_shape=jax.ShapeDtypeStruct((rows, share), BF16),
        in_specs=[vmem, hbm, hbm, vmem, hbm, hbm, vmem, vmem, vmem, hbm, hbm, hbm],
        out_specs=vmem,
        scratch_shapes=[
            pltpu.VMEM((rows, cache, HD), BF16),
            pltpu.VMEM((rows, cache, HD), BF16),
            pltpu.VMEM((4, share, 4 * share), BF16),
            pltpu.VMEM((16 * share, hidden_units), BF16),
            pltpu.VMEM((16 * share, hidden_units), BF16),
            pltpu.VMEM((4, hidden_units, 4 * share), BF16),
            pltpu.VMEM((rows, share), BF16),
            pltpu.VMEM((4, 4, rows, share), BF16),
            pltpu.VMEM((2, 2, 3, 4, step, share), BF16),
            pltpu.VMEM((2, 2, 3, step, share), BF16),
            pltpu.VMEM((2, 2, 4, step, share), BF16),
            pltpu.VMEM((4, 4, slots, share), BF16),
            pltpu.VMEM((4, 4, quarter, share), BF16),
            pltpu.VMEM((4, 2, 4, quarter, share), BF16),
            pltpu.VMEM((4, 3, quarter, share), BF16),
            pltpu.VMEM((4, 4, slots, share), BF16),
            pltpu.VMEM((8, PAD, share), BF16),
            pltpu.VMEM((7, PAD, share), BF16),
            pltpu.VMEM((8, PAD, share), BF16),
            pltpu.VMEM((8, PAD, share), BF16),
            pltpu.VMEM((slots, share), F32),
            pltpu.VMEM((slots, hidden_units), F32),
            pltpu.VMEM((slots, hidden_units), F32),
            pltpu.VMEM((slots, 128), F32),
            pltpu.VMEM((slots, hidden_units), BF16),
            pltpu.SemaphoreType.DMA((10,)),
            pltpu.SemaphoreType.DMA((1,)),
            pltpu.SemaphoreType.DMA((N_SEMS,)),
        ],
        compiler_params=pltpu.CompilerParams(
            collective_id=0, has_side_effects=True, vmem_limit_bytes=56 * 1024 * 1024
        ),
    )(
        queries, key_cache, value_cache, lengths.reshape(1, rows), out_proj, residual, norm_gain.reshape(1, 16 * share),
        expert_ids.T, gate_weights.T, w_gate, w_up, w_down,
    )


def solution(mesh):
    placed = (
        P("dp", "tensor"),
        P("dp", "tensor", None, None),
        P("dp", "tensor", None, None),
        P("dp"),
        P("tensor", None),
        P("dp", None),
        P(),
        P("dp", None),
        P("dp", None),
        P("dp", None, "tensor"),
        P("dp", None, "tensor"),
        P("dp", "tensor", None),
    )
    return jax.shard_map(
        local, mesh=mesh, in_specs=placed, out_specs=P("dp", "tensor"), check_vma=False
    )
```

time: 268 us -> 67.3 us (0.25)
  waiting for transfers between devices: 169 us -> 0 us
  Pallas kernels: 0 us -> 64.3 us
  blocking collectives: 35.7 us -> 0 us
  matrix products: 24.9 us -> 0 us
  between operations: 13.5 us -> 0.01 us
  local copies, waits for them, and re-layouts: 10.6 us -> 2.75 us
  starting transfers between devices: 6.74 us -> 0 us
  other arithmetic: 6.54 us -> 0 us
    psum x1 -> x0, waiting for transfers between devices: 89.6 us -> none  [local(): hidden = residual.astype(jnp.float32) + lax.psum(partial_value, 'tensor')]
    reduce_scatter x1 -> x0, waiting for transfers between devices: 74.3 us -> none  [local(): lax.psum_scatter(expert_terms, 'tensor', scatter_dimension=1, tiled=True)]
    pallas_call x0 -> x1, Pallas kernels: none -> 64.3 us  [local(): pl.pallas_call(kernel, out_shape=jax.ShapeDtypeStruct((rows, share), BF16...]
    all_to_all x1 -> x0, blocking collectives: 35.7 us -> none  [local(): lax.all_to_all(outgoing, 'dp', split_axis=0, concat_axis=0, tiled=True)]
    dot_general x7 -> x0, matrix products: 24.9 us -> none  [the longest x1 10.1 us: local(): expert_terms = jnp.dot(active, down_mat, preferred_element_type=jnp.float32)]
    all_to_all x1 -> x0, starting transfers between devices: 6.7 us -> none  [local(): lax.all_to_all(result.reshape(experts, capacity, share_width), 'dp', spli...]
    all_to_all x1 -> x0, waiting for transfers between devices: 5.42 us -> none  [local(): lax.all_to_all(result.reshape(experts, capacity, share_width), 'dp', spli...]
    convert_element_type x5 -> x0, other arithmetic: 3.49 us -> none  [the longest x1 1.65 us: local(): lax.psum_scatter(expert_terms, 'tensor', scatter_dimension=1, tiled=True)]
  transfers between devices with their start and end apart: 3 -> 0, of which waited for: 3 -> 0; matrix products, arithmetic and copies ran while one was open for 0% -> 0% of each run, Pallas kernels for 0% -> 0%
where the time goes in v1:
time: 67.3 us; the launch traced here: 67 us
  Pallas kernels  64.3 us (96%)
  local copies, waits for them, and re-layouts  2.75 us (4%)
    pallas_call x1, Pallas kernels, local(): pl.pallas_call(kernel, out_shape=jax.ShapeDtypeStruct((rows, share), BF16...  64.3 us
    unnamed x1, local copies, waits for them, and re-layouts  1.42 us

profile of v1, /device:TPU:1, one launch (start us, length us, event | category | flops | bytes accessed | tf_op | source)
XLA Modules:
  0.0 67.0 jit_solution(12291653839781948758)
XLA Ops:
  0.0 1.3 %reshape.7.gain = bf16[1,6144]{1,0:T(2,128)(2,1)} reshape(bf16[6144]{0:T(1024)(128)(2,1)} %param.18) | data formatting | bytes 24576 | tf_op jit(solution)/shard_map/reshape | solution.py:540
  1.3 64.3 %shard_map.118 = bf16[64,384]{1,0:T(8,128)(2,1)} custom-call(bf16[64,384]{1,0:T(8,128)(2,1)} %queries.1, bf16[64,1,128,128]{3,2,1,0:T(8,128)(2,1)} %keys_hbm.1, bf16[64,1,128,128]{3,2,1,0:T(8,128)(2,1)} %values_hbm.1, s32[1,64]{1,0:T(1,128)} %bitcast.5, bf16[384,6144]{1,0:T(8,128)(2,1)} %wo_hbm.1, bf16[64,6144]{1,0:T(8,128)(2,1)} %res_hbm.1, ...), custom_call_target="tpu_custom_call" | custom-call | tf_op jit(solution)/shard_map/pallas_call | solution.py:501
  65.6 1.4 %copy.14 = bf16[64,384]{1,0:T(8,128)(2,1)} copy(bf16[64,384]{1,0:T(8,128)(2,1)} %shard_map.118) | data formatting | bytes 98304

commit v2 on v1

--- a/solution.py
+++ b/solution.py
@@ -379,7 +379,7 @@
     )
     to_send[...] = picked.astype(BF16).reshape(8, PAD, share)
 
-    for k in (2, 3, 6, 7, 1, 4, 5):
+    for k in (4, 5, 2, 3, 6, 7, 1):
         links.send("d", to_send.at[k], landed.at[k - 1], k)
     quarter = 2 * CAP
     gathers = [

time: 67.3 us -> 67.3 us (level)
  no operation moved by 1% of the time
where the time goes in v2:
time: 67.3 us; the launch traced here: 67 us
  Pallas kernels  64.3 us (96%)
  local copies, waits for them, and re-layouts  2.75 us (4%)
    pallas_call x1, Pallas kernels, local(): pl.pallas_call(kernel, out_shape=jax.ShapeDtypeStruct((rows, share), BF16...  64.3 us
    unnamed x1, local copies, waits for them, and re-layouts  1.42 us

profile of v2, /device:TPU:1, one launch (start us, length us, event | category | flops | bytes accessed | tf_op | source)
XLA Modules:
  0.0 67.0 jit_solution(4087532724033208338)
XLA Ops:
  0.0 1.3 %reshape.7.gain = bf16[1,6144]{1,0:T(2,128)(2,1)} reshape(bf16[6144]{0:T(1024)(128)(2,1)} %param.18) | data formatting | bytes 24576 | tf_op jit(solution)/shard_map/reshape | solution.py:540
  1.3 64.3 %shard_map.118 = bf16[64,384]{1,0:T(8,128)(2,1)} custom-call(bf16[64,384]{1,0:T(8,128)(2,1)} %queries.1, bf16[64,1,128,128]{3,2,1,0:T(8,128)(2,1)} %keys_hbm.1, bf16[64,1,128,128]{3,2,1,0:T(8,128)(2,1)} %values_hbm.1, s32[1,64]{1,0:T(1,128)} %bitcast.5, bf16[384,6144]{1,0:T(8,128)(2,1)} %wo_hbm.1, bf16[64,6144]{1,0:T(8,128)(2,1)} %res_hbm.1, ...), custom_call_target="tpu_custom_call" | custom-call | tf_op jit(solution)/shard_map/pallas_call | solution.py:501
  65.6 1.4 %copy.14 = bf16[64,384]{1,0:T(8,128)(2,1)} copy(bf16[64,384]{1,0:T(8,128)(2,1)} %shard_map.118) | data formatting | bytes 98304

commit v3 on v2

--- a/solution.py
+++ b/solution.py
@@ -13,7 +13,7 @@
 EPSILON = 1e-05
 F32 = jnp.float32
 BF16 = jnp.bfloat16
-N_SEMS = 8 + 28 + 36 + 1 + 1
+N_SEMS = 8 + 28 + 36 + 2 + 1
 
 ORDER = (
     (2, 2), (1, 2), (3, 2), (2, 1), (2, 3), (1, 1), (1, 3), (3, 1), (3, 3),
@@ -379,8 +379,8 @@
     )
     to_send[...] = picked.astype(BF16).reshape(8, PAD, share)
 
-    for k in (4, 5, 2, 3, 6, 7, 1):
-        links.send("d", to_send.at[k], landed.at[k - 1], k)
+    for k in (1, 4, 5, 2, 3, 6, 7):
+        links.send("d" if k > 1 else "d1", to_send.at[k], landed.at[k - 1], k)
     quarter = 2 * CAP
     gathers = [
         Gather(held, links, index, quarter, axes, side)
@@ -388,10 +388,14 @@
     ]
 
     rows_f32[0:CAP, :] = f32(to_send[0])[:CAP]
-    links.arrived("d", landed)
-    for k in range(1, 8):
+    links.arrived("d1", landed.at[0])
+    rows_f32[CAP:2 * CAP, :] = f32(landed[0])[:CAP]
+    held[0, 0, 0:quarter, :] = rows_f32[0:quarter, :].astype(BF16)
+    gathers[0].own()
+    links.arrived("d", landed.at[pl.ds(1, 6)])
+    for k in range(2, 8):
         rows_f32[k * CAP:(k + 1) * CAP, :] = f32(landed[k - 1])[:CAP]
-    held[0, 0] = rows_f32[...].astype(BF16)
+    held[0, 0, quarter:4 * quarter, :] = rows_f32[quarter:4 * quarter, :].astype(BF16)
 
     def consume(i, j):
         values_f32 = f32(held[i, j])
@@ -404,7 +408,7 @@
         acc_gate[...] += jnp.dot(scaled, wg[block_rows(i, j), :], preferred_element_type=F32)
         acc_up[...] += jnp.dot(scaled, wu[block_rows(i, j), :], preferred_element_type=F32)
 
-    for each in gathers:
+    for each in gathers[1:]:
         each.own()
     wait("wg", wg)
     wait("wu", wu)

time: 67.3 us -> 66.4 us (0.987)
  Pallas kernels: 64.3 us -> 63.4 us
    pallas_call x1, Pallas kernels: 64.3 us -> 63.4 us  [local(): pl.pallas_call(kernel, out_shape=jax.ShapeDtypeStruct((rows, share), BF16...]
where the time goes in v3:
time: 66.4 us; the launch traced here: 66.2 us
  Pallas kernels  63.4 us (95%)
  local copies, waits for them, and re-layouts  2.75 us (4%)
    pallas_call x1, Pallas kernels, local(): pl.pallas_call(kernel, out_shape=jax.ShapeDtypeStruct((rows, share), BF16...  63.4 us
    unnamed x1, local copies, waits for them, and re-layouts  1.42 us

profile of v3, /device:TPU:1, one launch (start us, length us, event | category | flops | bytes accessed | tf_op | source)
XLA Modules:
  0.0 66.2 jit_solution(9955506445840997638)
XLA Ops:
  0.0 1.3 %reshape.7.gain = bf16[1,6144]{1,0:T(2,128)(2,1)} reshape(bf16[6144]{0:T(1024)(128)(2,1)} %param.18) | data formatting | bytes 24576 | tf_op jit(solution)/shard_map/reshape | solution.py:544
  1.3 63.4 %shard_map.118 = bf16[64,384]{1,0:T(8,128)(2,1)} custom-call(bf16[64,384]{1,0:T(8,128)(2,1)} %queries.1, bf16[64,1,128,128]{3,2,1,0:T(8,128)(2,1)} %keys_hbm.1, bf16[64,1,128,128]{3,2,1,0:T(8,128)(2,1)} %values_hbm.1, s32[1,64]{1,0:T(1,128)} %bitcast.5, bf16[384,6144]{1,0:T(8,128)(2,1)} %wo_hbm.1, bf16[64,6144]{1,0:T(8,128)(2,1)} %res_hbm.1, ...), custom_call_target="tpu_custom_call" | custom-call | tf_op jit(solution)/shard_map/pallas_call | solution.py:505
  64.7 1.4 %copy.14 = bf16[64,384]{1,0:T(8,128)(2,1)} copy(bf16[64,384]{1,0:T(8,128)(2,1)} %shard_map.118) | data formatting | bytes 98304
